TPU v7x, 32 devices: a whole 2x2x4 slice. The times are simulated.
32 devices in a mesh: energy: 8 (over z, y), seg: 4 (over x, core).
Axes of the slice: x: 2, y: 2, z: 4, core: 2. Of those that a mesh axis runs over, the one named last changes fastest.
Arguments:
- lesser: float32 [32, 8, 2, 256, 256], P('energy', 'seg'), may hold values from -6 to 6
- greater: float32 [32, 8, 2, 256, 256], P('energy', 'seg'), may hold values from -6 to 6
- coupling_low: float32 [32, 8, 2, 256, 256], P('energy', 'seg'), may hold values from -0.125 to 0.125
- coupling_up: float32 [32, 8, 2, 256, 256], P('energy', 'seg'), may hold values from -0.125 to 0.125
Outputs:
- polarization: float32 [32, 8, 2, 256, 256], P('energy', 'seg')
- lesser_full: float32 [32, 8, 2, 256, 256], P('energy', 'seg')
All inputs are finite; a program needn't handle non-finite values.
Results may differ from a plain program's by a relative error of at most 0.0001.
Values sent between devices are 32-bit elements; how exact they have to be, the bound alone decides.
A program may use at most 128 MiB of HBM per device.

v0:
```python
import math

import jax
import jax.numpy as jnp
from jax import lax
from jax.sharding import PartitionSpec as P


def carried_in(part, axis, combine, identity, reverse):
    count = lax.axis_size(axis)
    place = lax.axis_index(axis)
    ahead = count - 1 - place if reverse else place
    gathered = lax.all_gather(part, axis)
    state = jnp.zeros_like(part) + jnp.asarray(identity, part.dtype)

    def one(turn, state):
        source = count - 1 - turn if reverse else turn
        return combine(state, lax.dynamic_index_in_dim(gathered, source, 0, False))

    return lax.fori_loop(0, ahead, one, state)


def complex_product(former, latter):

    def multiply(one_part, two_part):
        return jnp.einsum("...ij,...jk->...ik", one_part, two_part, precision=lax.Precision.HIGHEST)

    real_part = multiply(former[..., 0, :, :], latter[..., 0, :, :]) - multiply(
        former[..., 1, :, :], latter[..., 1, :, :]
    )
    imag_part = multiply(former[..., 0, :, :], latter[..., 1, :, :]) + multiply(
        former[..., 1, :, :], latter[..., 0, :, :]
    )
    return jnp.stack([real_part, imag_part], axis=-3)


def chain_combine(earlier, later):
    return complex_product(later, earlier)


def transform(table, values):
    return jnp.einsum("mf,mx->fx", table, values, precision=lax.Precision.HIGHEST)


def untransform(table, values):
    return jnp.einsum("mf,fx->mx", table, values, precision=lax.Precision.HIGHEST)


def correlate(pair_rows):
    lesser_rows, conj_rows = pair_rows
    energies_all = lesser_rows.shape[0]
    length = 2 * energies_all
    inner_shape = (lesser_rows.shape[1],) + lesser_rows.shape[3:]
    positions = jnp.arange(energies_all, dtype=jnp.int32)
    frequency = jnp.arange(length, dtype=jnp.int32)
    phase = positions[:, None] * frequency[None, :] % length
    angles = phase.astype(jnp.float32) * (2.0 * math.pi / length)
    cosine = jnp.cos(angles)
    sine = jnp.sin(angles)
    lesser_re = lesser_rows[:, :, 0].reshape(energies_all, -1)
    lesser_im = lesser_rows[:, :, 1].reshape(energies_all, -1)
    conj_re = conj_rows[:, :, 0].reshape(energies_all, -1)
    conj_im = conj_rows[:, :, 1].reshape(energies_all, -1)
    freq_lesser_re = transform(cosine, lesser_re) + transform(sine, lesser_im)
    freq_lesser_im = transform(cosine, lesser_im) - transform(sine, lesser_re)
    freq_conj_re = transform(cosine, conj_re) - transform(sine, conj_im)
    freq_conj_im = transform(cosine, conj_im) + transform(sine, conj_re)
    prod_real = freq_lesser_re * freq_conj_re - freq_lesser_im * freq_conj_im
    prod_imag = freq_lesser_re * freq_conj_im + freq_lesser_im * freq_conj_re
    scale_factor = 1.0 / (length * math.sqrt(energies_all))
    out_real = (untransform(cosine, prod_real) - untransform(sine, prod_imag)) * scale_factor
    out_imag = (untransform(cosine, prod_imag) + untransform(sine, prod_real)) * scale_factor
    return jnp.stack(
        [
            out_real.reshape((energies_all,) + inner_shape),
            out_imag.reshape((energies_all,) + inner_shape),
        ],
        axis=2,
    )


def on_device(lesser, greater, coupling_low, coupling_up):
    here_energies = lesser.shape[0]
    here_segments = lesser.shape[1]
    block_size = lesser.shape[-1]
    eye_block = jnp.eye(block_size, dtype=jnp.float32)
    identity = jnp.broadcast_to(
        jnp.stack([eye_block, jnp.zeros_like(eye_block)]),
        (here_energies, 2, block_size, block_size),
    )
    corner_low = coupling_low + identity[:, None]
    corner_up = coupling_up + identity[:, None]
    low_total = corner_low[:, 0]
    segment = 1
    low_total = complex_product(corner_low[:, segment], low_total)
    up_total = corner_up[:, here_segments - 1]
    segment = 0
    up_total = complex_product(corner_up[:, segment], up_total)
    left_prefix = carried_in(low_total, "seg", chain_combine, identity, False)
    right_prefix = carried_in(up_total, "seg", chain_combine, identity, True)
    lefts = [left_prefix]
    segment = 1
    lefts.append(complex_product(corner_low[:, segment - 1], lefts[-1]))
    rights = [right_prefix]
    segment = 0
    rights.insert(0, complex_product(corner_up[:, segment + 1], rights[0]))
    transfer = jnp.stack(
        [complex_product(lefts[segment], rights[segment]) for segment in range(here_segments)],
        axis=1,
    )
    lesser_full = lesser + transfer
    conj_greater = jnp.stack(
        [greater[:, :, 0] + transfer[:, :, 0], transfer[:, :, 1] - greater[:, :, 1]], axis=2
    )
    element_data = (
        lax.all_to_all(lesser_full, "energy", split_axis=3, concat_axis=0, tiled=True),
        lax.all_to_all(conj_greater, "energy", split_axis=3, concat_axis=0, tiled=True),
    )
    polarization = lax.all_to_all(
        correlate(element_data), "energy", split_axis=0, concat_axis=3, tiled=True
    )
    return (polarization, lesser_full)


def solution(mesh):
    return jax.shard_map(
        on_device,
        mesh=mesh,
        in_specs=(
            P("energy", "seg", None, None, None),
            P("energy", "seg", None, None, None),
            P("energy", "seg", None, None, None),
            P("energy", "seg", None, None, None),
        ),
        out_specs=(P("energy", "seg", None, None, None), P("energy", "seg", None, None, None)),
        check_vma=False,
    )
```

profile of v0, /device:TPU:2, one launch (start us, length us, event | category | flops | bytes accessed | tf_op | source)
XLA Modules:
  0.0 542.8 jit_solution(259515050557672785)
XLA Ops:
  7.3 4.1 copy_add_fusion
  11.4 2.0 slice_bitcast_fusion.13
  18.0 1.5 pad_maximum_fusion.6
  19.6 2.5 fusion.63
  25.6 1.6 pad_maximum_fusion.5
  27.2 5.5 %fusion.158 = (f32[4,2,1,256,256]{4,3,2,1,0:T(8,128)}, f32[4,2,1,256,256]{4,3,2,1,0:T(8,128)}) fusion(f32[4,2,2,256,256]{4,3,2,1,0:T(8,128)} %param.9), kind=kLoop, calls=%fused_computation.208 | loop fusion | bytes 8388608 | tf_op jit(solution)/shard_map/slice | solution.py:113
  32.7 45.3 %all-gather.7.cloned.1.call-done = f32[16,2,256,256]{3,2,0,1:T(8,128)} async-done(((f32[4,2,256,256]{3,2,0,1:T(8,128)}), f32[16,2,256,256]{3,2,0,1:T(8,128)}) %all-gather.7.cloned.1.call-update) | async-done | bytes 8388624 | tf_op jit(solution)/shard_map/all_gather | solution.py:13
  78.2 6.8 %while.23 = (s32[]{:T(128)}, f32[4,2,256,256]{3,2,0,1:T(8,128)S(1)}, s32[]{:T(128)}, f32[4,4,2,256,256]{4,3,1,0,2:T(8,128)}, s32[]{:T(128)}, /*index=5*/s32[]{:T(128)}, s32[]{:T(128)}, s32[]{:T(128)}) while((s32[]{:T(128)}, f32[4,2,256,256]{3,2,0,1:T(8,128)S(1)}, s32[]{:T(128)}, f32[4,4,2,256,256]{4,3,1,0,2:T(8,128)}, s32[]{:T(128)}, ...), condition=%wide.region_3.4_spmd, body=%wide.region_2.3_spmd.sunk | while | flops 3222274048 | bytes 23068816 | solution.py:20
  78.5 1.7 dynamic-slice_bitcast_fusion.5
  85.1 4.2 fusion.47
  89.3 2.1 fusion.54
  91.4 46.5 %all-gather.5.cloned.1.call-done = f32[16,2,256,256]{3,2,0,1:T(8,128)} async-done(((f32[4,2,256,256]{3,2,0,1:T(8,128)}), f32[16,2,256,256]{3,2,0,1:T(8,128)}) %all-gather.5.cloned.1.call-update) | async-done | bytes 8388624 | tf_op jit(solution)/shard_map/all_gather | solution.py:13
  138.1 21.9 %while.22 = (s32[]{:T(128)}, f32[4,2,256,256]{3,2,0,1:T(8,128)S(1)}, s32[]{:T(128)}, f32[4,4,2,256,256]{4,3,1,0,2:T(8,128)}, s32[]{:T(128)}, /*index=5*/s32[]{:T(128)}, s32[]{:T(128)}) while((s32[]{:T(128)}, f32[4,2,256,256]{3,2,0,1:T(8,128)S(1)}, s32[]{:T(128)}, f32[4,4,2,256,256]{4,3,1,0,2:T(8,128)}, s32[]{:T(128)}, /*index=5*/s32[]{:T(128)}, ...), condition=%wide.region_1.2_spmd, body=%wide.region_0.1_spmd.sunk | while | flops 3222274048 | bytes 23068796 | solution.py:20
  138.1 1.7 dynamic-slice_bitcast_fusion.4
  144.7 1.7 dynamic-slice_bitcast_fusion.4
  160.0 2.5 fusion.57
  174.2 1.6 fusion.34
  179.5 2.2 copy-done.12
  183.4 4.7 copy.49
  188.1 5.8 %all-to-all-start.1 = ((f32[4,2,2,256,256]{4,0,2,1,3:T(4,128)}), f32[4,2,2,256,256]{4,0,2,1,3:T(4,128)}, u32[]{:S(2)}, u32[]{:S(2)}) async-start(f32[4,2,2,256,256]{4,0,2,1,3:T(4,128)} %copy.49), calls=%async_computation.1 | async-start | bytes 8388608 | tf_op jit(solution)/shard_map/all_to_all | solution.py:117
  193.9 3.4 fusion.26
  197.2 2.0 copy-done.7
  199.2 4.7 copy.44
  203.9 79.8 %all-to-all-done.1 = f32[4,2,2,256,256]{4,0,2,1,3:T(4,128)} async-done(((f32[4,2,2,256,256]{4,0,2,1,3:T(4,128)}), f32[4,2,2,256,256]{4,0,2,1,3:T(4,128)}, u32[]{:S(2)}, u32[]{:S(2)}) %all-to-all-start.1) | async-done | bytes 4194336 | tf_op jit(solution)/shard_map/all_to_all | solution.py:117
  283.7 8.6 %all-to-all-start = ((f32[4,2,2,256,256]{4,0,2,1,3:T(4,128)}), f32[4,2,2,256,256]{4,0,2,1,3:T(4,128)}, u32[]{:S(2)}, u32[]{:S(2)}) async-start(f32[4,2,2,256,256]{4,0,2,1,3:T(4,128)} %copy.44), calls=%async_computation | async-start | bytes 8388608 | tf_op jit(solution)/shard_map/all_to_all | solution.py:116
  292.3 4.6 copy.50
  298.1 1.2 copy.63
  299.4 1.2 copy.62
  300.6 3.6 fusion.95
  304.2 5.2 fusion.99
  309.5 5.6 %convolution_add_fusion.2 = f32[64,16384]{1,0:T(8,128)} fusion(f32[64,16384]{1,0:T(8,128)S(1)} %fusion.95, f32[32,16384]{1,0:T(8,128)S(1)} %bitcast.261), kind=kOutput, calls=%fused_computation.36 | convolution fusion | flops 403730432 | bytes 10485760 | tf_op jit(solution)/shard_map/mf,mx->fx/dot_general | solution.py:42
  315.1 72.0 %all-to-all-done = f32[4,2,2,256,256]{4,0,2,1,3:T(4,128)} async-done(((f32[4,2,2,256,256]{4,0,2,1,3:T(4,128)}), f32[4,2,2,256,256]{4,0,2,1,3:T(4,128)}, u32[]{:S(2)}, u32[]{:S(2)}) %all-to-all-start) | async-done | bytes 4194336 | tf_op jit(solution)/shard_map/all_to_all | solution.py:116
  387.1 4.6 copy.45
  392.6 1.2 copy.60
  393.8 3.6 fusion.101
  398.6 3.8 fusion.97
  402.4 5.2 convolution_add_fusion.3
  407.6 5.3 convolution_subtract_fusion.3
  412.9 7.1 %multiply_subtract_fusion = (f32[64,16384]{1,0:T(8,128)S(1)}, f32[64,16384]{1,0:T(8,128)S(1)}) fusion(f32[64,16384]{1,0:T(8,128)S(1)} %copy-done.11, f32[64,16384]{1,0:T(8,128)} %convolution_add_fusion.3, f32[64,16384]{1,0:T(8,128)} %convolution_subtract_fusion.3, f32[64,16384]{1,0:T(8,128)S(1)} %fusion.97, f32[32,16384]{1,0:T(8,128)S(1)} %bitcast.265), kind=kOutput, calls=%fused_computation.55 | convolution fusion | flops 410021888 | bytes 27262976 | tf_op jit(solution)/shard_map/mf,mx->fx/dot_general | solution.py:42
  419.9 2.2 fusion.91
  422.1 2.2 fusion.93
  424.3 2.3 fusion.24
  427.3 2.4 fusion.25
  430.3 2.3 pad_maximum_fusion.4
  432.7 4.6 all-to-all-start.2
  437.2 4.6 copy.55
  441.8 89.1 %all-to-all-done.2 = f32[32,2,2,32,256]{4,3,1,2,0:T(8,128)} async-done(((f32[32,2,2,32,256]{4,3,1,2,0:T(8,128)}), f32[32,2,2,32,256]{4,3,1,2,0:T(8,128)}, u32[]{:S(2)}, u32[]{:S(2)}) %all-to-all-start.2) | async-done | bytes 4194336 | tf_op jit(solution)/shard_map/all_to_all | solution.py:119
  531.0 4.8 copy.54
  (83 shorter events, 44.4 us)
Async XLA Ops:
  7.2 70.9 %all-gather.7.cloned.1.call-start = ((), (), s32[]{:S(2)}) async-start(), calls=%async_computation.4 | async-start | bytes 10485760 | tf_op jit(solution)/shard_map/all_gather | solution.py:13
  13.3 3.5 copy-start.4
  13.3 11.1 %copy-start.2 = (f32[4,2,256,256]{3,2,0,1:T(8,128)}, f32[4,2,256,256]{3,2,0,1:T(8,128)S(1)}, u32[]{:S(2)}) copy-start(f32[4,2,256,256]{3,2,0,1:T(8,128)S(1)} %get-tuple-element.155) | copy-start | bytes 6291460
  19.5 118.4 %all-gather.5.cloned.1.call-start = ((), (), s32[]{:S(2)}) async-start(), calls=%async_computation.3 | async-start | bytes 10485760 | tf_op jit(solution)/shard_map/all_gather | solution.py:13
  19.6 2.5 copy-start.9
  85.1 6.4 %copy-start = (f32[4,2,256,256]{3,2,0,1:T(8,128)}, f32[4,2,256,256]{3,2,0,1:T(8,128)S(1)}, u32[]{:S(2)}) copy-start(f32[4,2,256,256]{3,2,0,1:T(8,128)S(1)} %get-tuple-element.82) | copy-start | bytes 6291460
  85.1 4.2 copy-start.5
  160.0 2.5 copy-start.3
  163.7 1.6 copy-start.1
  166.4 1.6 copy-start.6
  166.4 1.8 copy-start.15
  169.5 1.2 copy-start.14
  179.4 2.3 copy-start.12
  179.4 3.0 copy-start.13
  179.5 3.5 copy-start.8
  188.1 95.6 %all-to-all-start.1 = ((f32[4,2,2,256,256]{4,0,2,1,3:T(4,128)}), f32[4,2,2,256,256]{4,0,2,1,3:T(4,128)}, u32[]{:S(2)}, u32[]{:S(2)}) async-start(f32[4,2,2,256,256]{4,0,2,1,3:T(4,128)} %copy.49), calls=%async_computation.1 | async-start | bytes 8388608 | tf_op jit(solution)/shard_map/all_to_all | solution.py:117
  197.2 2.0 copy-start.7
  283.7 103.4 %all-to-all-start = ((f32[4,2,2,256,256]{4,0,2,1,3:T(4,128)}), f32[4,2,2,256,256]{4,0,2,1,3:T(4,128)}, u32[]{:S(2)}, u32[]{:S(2)}) async-start(f32[4,2,2,256,256]{4,0,2,1,3:T(4,128)} %copy.44), calls=%async_computation | async-start | bytes 8388608 | tf_op jit(solution)/shard_map/all_to_all | solution.py:116
  402.4 5.2 copy-start.10
  407.6 5.3 copy-start.11
  432.7 98.3 %all-to-all-start.2 = ((f32[32,2,2,32,256]{4,3,1,2,0:T(8,128)}), f32[32,2,2,32,256]{4,3,1,2,0:T(8,128)}, u32[]{:S(2)}, u32[]{:S(2)}) async-start(f32[32,2,2,32,256]{4,3,1,2,0:T(8,128)} %pad_maximum_fusion.4), calls=%async_computation.2 | async-start | bytes 8388608 | tf_op jit(solution)/shard_map/all_to_all | solution.py:119
Sparse Core Ops, SparseCore 0:
  19.7 58.3 all-gather.6
  79.6 58.2 all-gather.4
where the time goes:
time: 548 us; the launch traced here: 543 us
  waiting for transfers between devices  333 us (61%)
  matrix products  97.1 us (18%)
  local copies, waits for them, and re-layouts  55.3 us (10%)
  starting transfers between devices  19.1 us (3%)
  between operations  14.8 us (3%)
  other arithmetic  14.6 us (3%)
  loops' own time  9.2 us (2%)
    all_gather x2, waiting for transfers between devices, carried_in(): gathered = lax.all_gather(part, axis)  91.8 us
    all_to_all x1, waiting for transfers between devices, on_device(): lax.all_to_all(correlate(element_data), 'energy', split_axis=0, concat_ax...  89.1 us
    all_to_all x1, waiting for transfers between devices, on_device(): lax.all_to_all(conj_greater, 'energy', split_axis=3, concat_axis=0, tiled...  79.8 us
    all_to_all x1, waiting for transfers between devices, on_device(): lax.all_to_all(lesser_full, 'energy', split_axis=3, concat_axis=0, tiled=...  72 us
    dot_general x36, matrix products, multiply(): jnp.einsum('...ij,...jk->...ik', one_part, two_part, precision=lax.Precis...  48.7 us
    dot_general x8, matrix products, transform(): jnp.einsum('mf,mx->fx', table, values, precision=lax.Precision.HIGHEST)  39.3 us
    unnamed x39, local copies, waits for them, and re-layouts  16.7 us
  transfers between devices with their start and end apart: 5, of which 5 were waited for; matrix products, arithmetic and copies ran while one was open for 11% of the time, Pallas kernels for 0%

commit v1 on v0

v1 whole, which is shorter than its diff:
```python
import functools
import math

import jax
import jax.numpy as jnp
from jax import lax
from jax.experimental import pallas as pl
from jax.experimental.pallas import tpu as pltpu
from jax.sharding import PartitionSpec as P

MESH = pl.DeviceIdType.MESH
ROWS = 16
LAG = 4
WINDOW = 3


def complex_product(former, latter):

    def multiply(one_part, two_part):
        return jnp.einsum("...ij,...jk->...ik", one_part, two_part, precision=lax.Precision.HIGH)

    real_part = multiply(former[..., 0, :, :], latter[..., 0, :, :]) - multiply(
        former[..., 1, :, :], latter[..., 1, :, :]
    )
    imag_part = multiply(former[..., 0, :, :], latter[..., 1, :, :]) + multiply(
        former[..., 1, :, :], latter[..., 0, :, :]
    )
    return jnp.stack([real_part, imag_part], axis=-3)


def swap_pairs(part):
    return lax.ppermute(part, "seg", [(0, 1), (1, 0), (2, 3), (3, 2)])


def chain(coupling_low, coupling_up):
    place = lax.axis_index("seg")
    even = place % 2 == 0
    outer = (place == 0) | (place == 3)
    energies = coupling_low.shape[0]
    block_size = coupling_low.shape[-1]
    eye_block = jnp.eye(block_size, dtype=jnp.float32)
    identity = jnp.broadcast_to(
        jnp.stack([eye_block, jnp.zeros_like(eye_block)]), (energies, 2, block_size, block_size)
    )
    low = [coupling_low[:, s] + identity for s in range(2)]
    up = [coupling_up[:, s] + identity for s in range(2)]
    low_total = complex_product(low[1], low[0])
    up_total = complex_product(up[0], up[1])
    near = swap_pairs(jnp.where(even, low_total, up_total))
    pair = complex_product(jnp.where(even, up_total, low_total), near)
    half = energies // 2
    to_outer = lax.ppermute(pair[:half], "seg", [(1, 3), (2, 0)])
    to_inner = lax.ppermute(pair[half:], "seg", [(1, 2), (2, 1)])
    mine = jnp.where(outer, to_outer, to_inner)
    other = swap_pairs(mine)
    far = jnp.concatenate([jnp.where(outer, mine, other), jnp.where(outer, other, mine)], axis=0)
    both = complex_product(near, far)
    left = jnp.where(
        place == 0, identity, jnp.where(place == 1, near, jnp.where(place == 2, far, both))
    )
    right = jnp.where(
        place == 0, both, jnp.where(place == 1, far, jnp.where(place == 2, near, identity))
    )
    first = complex_product(left, complex_product(up[1], right))
    second = complex_product(complex_product(low[0], left), right)
    return jnp.stack([first, second], axis=1)


def block_terms(lesser_ref, greater_ref, rows, columns, later):
    size = lesser_ref.shape[0]
    l_re, l_im = lesser_ref[:, 0, rows, columns], lesser_ref[:, 1, rows, columns]
    g_re, g_im = greater_ref[:, 0, rows, columns], greater_ref[:, 1, rows, columns]
    terms = []
    for shift in range(size):
        if later and shift == 0:
            terms.append(None)
            continue
        if later:
            here, there = slice(0, shift), slice(size - shift, size)
        else:
            here, there = slice(shift, size), slice(0, size - shift)
        real_part = l_re[here] * g_re[there] + l_im[here] * g_im[there]
        imag_part = l_im[here] * g_re[there] - l_re[here] * g_im[there]
        terms.append((jnp.sum(real_part, axis=0), jnp.sum(imag_part, axis=0)))
    return terms


def correlate_block(out_ref, pairs, rows, columns, scale):
    total = None
    for lesser_ref, greater_ref, later in pairs:
        terms = block_terms(lesser_ref, greater_ref, rows, columns, later)
        if total is None:
            total = terms
        else:
            total = [
                old if new is None else (old[0] + new[0], old[1] + new[1])
                for old, new in zip(total, terms)
            ]
    for shift, (real_part, imag_part) in enumerate(total):
        out_ref[shift, 0, rows, columns] = real_part * scale
        out_ref[shift, 1, rows, columns] = imag_part * scale


def exchange_kernel(
    scale,
    lesser,
    greater,
    out,
    l_own,
    g_own,
    g_one,
    g_two,
    in_a,
    in_b,
    part,
    own_sem,
    y_send,
    y_recv,
    f_send,
    f_recv,
    o_send,
    o_recv,
    o_own,
):
    chunks, block, _, rows, width = l_own.shape
    share = block // 2
    per_segment = chunks // lesser.shape[1]
    half_rows = lesser.shape[3] // 2
    place = lax.axis_index("energy")
    line = place // 2
    side = place % 2
    partner = place + 1 - 2 * side

    def region(ref, chunk, half):
        start = pl.multiple_of(half * half_rows + (chunk % per_segment) * rows, rows)
        return ref.at[:, chunk // per_segment, :, pl.ds(start, rows), :]

    def remote(source, target, send, recv, device):
        return pltpu.make_async_remote_copy(
            src_ref=source,
            dst_ref=target,
            send_sem=send,
            recv_sem=recv,
            device_id={"energy": device},
            device_id_type=MESH,
        )

    def own_copy(which, chunk):
        source, target = ((lesser, l_own), (greater, g_own))[which]
        return pltpu.make_async_copy(
            region(source, chunk, side),
            target.at[chunk, pl.ds(side * share, share)],
            own_sem.at[which, chunk],
        )

    def side_copy(which, chunk):
        source, target = ((lesser, l_own), (greater, g_own))[which]
        return remote(
            region(source, chunk, 1 - side),
            target.at[chunk, pl.ds(side * share, share)],
            y_send.at[which, chunk],
            y_recv.at[which, chunk],
            partner,
        )

    def issue(chunk):
        for which in (1, 0):
            side_copy(which, chunk).start()
            own_copy(which, chunk).start()

    def ready(which, chunk):
        own_copy(which, chunk).wait()
        side_copy(which, chunk).wait_recv()

    def along(source, target, send, recv, chunk, device):
        return remote(source, target, f_send.at[send, chunk], f_recv.at[recv, chunk], device)

    def arrived(recv, chunk):
        target = (g_one, g_two, in_a, in_b)[recv].at[chunk]
        along(target, target, recv, recv, chunk, partner).wait_recv()

    def result_copy(result, chunk):
        return remote(
            result.at[pl.ds((1 - side) * share, share)],
            region(out, chunk, side),
            o_send.at[chunk],
            o_recv.at[chunk],
            partner,
        )

    def result_own(result, chunk):
        return pltpu.make_async_copy(
            result.at[pl.ds(side * share, share)], region(out, chunk, side), o_own.at[chunk]
        )

    def finish(result, chunk):
        result_copy(result, chunk).start()
        result_own(result, chunk).start()

    def tiles(body):
        columns = width // 128

        def one(index, carry):
            row = pl.multiple_of((index // columns) * 8, 8)
            column = pl.multiple_of((index % columns) * 128, 128)
            body(pl.ds(row, 8), pl.ds(column, 128))
            return carry

        lax.fori_loop(0, (rows // 8) * columns, one, 0)

    def correlate(chunk, *blocks):
        def body(row, column):
            for index, pairs in blocks:
                correlate_block(part.at[chunk, index], pairs, row, column, scale)

        tiles(body)

    def add_in(index, source, chunk):
        part[chunk, index] = part[chunk, index] + source[chunk]

    def sends(chunk):
        return (
            (along(g_own.at[chunk], g_one.at[chunk], 0, 0, chunk, place + 2),),
            (
                along(g_own.at[chunk], g_one.at[chunk], 0, 0, chunk, place + 2),
                along(g_one.at[chunk], g_two.at[chunk], 1, 1, chunk, place + 2),
                along(part.at[chunk, 0], in_a.at[chunk], 2, 2, chunk, place - 2),
            ),
            (
                along(part.at[chunk, 0], in_a.at[chunk], 0, 2, chunk, place - 2),
                along(part.at[chunk, 1], in_b.at[chunk], 1, 3, chunk, place - 2),
                along(part.at[chunk, 3], in_a.at[chunk], 2, 2, chunk, place + 2),
            ),
            (
                along(l_own.at[chunk], in_a.at[chunk], 0, 2, chunk, place - 2),
                along(g_own.at[chunk], in_b.at[chunk], 1, 3, chunk, place - 2),
            ),
        )

    def result_of(index, chunk):
        return in_a.at[chunk] if index == 3 else part.at[chunk, index]

    def forward(index, chunk):
        l_here, g_here = l_own.at[chunk], g_own.at[chunk]
        one, two = g_one.at[chunk], g_two.at[chunk]
        l_next, g_next = in_a.at[chunk], in_b.at[chunk]
        moves = sends(chunk)[index]
        if index == 0:
            ready(1, chunk)
            moves[0].start()
            ready(0, chunk)
            correlate(chunk, (0, [(l_here, g_here, False)]))
        elif index == 1:
            ready(1, chunk)
            moves[0].start()
            arrived(0, chunk)
            moves[1].start()
            ready(0, chunk)
            correlate(
                chunk,
                (0, [(l_here, g_here, False), (l_here, one, True)]),
                (1, [(l_here, one, False)]),
            )
        elif index == 2:
            ready(1, chunk)
            ready(0, chunk)
            for recv in (2, 3, 0, 1):
                arrived(recv, chunk)
            correlate(
                chunk,
                (
                    0,
                    [
                        (l_here, g_here, False),
                        (l_next, g_next, False),
                        (l_here, one, True),
                        (l_next, g_here, True),
                    ],
                ),
                (
                    1,
                    [
                        (l_here, one, False),
                        (l_next, g_here, False),
                        (l_here, two, True),
                        (l_next, one, True),
                    ],
                ),
                (2, [(l_here, two, False), (l_next, one, False), (l_next, two, True)]),
                (3, [(l_next, two, False)]),
            )
            for move in moves:
                move.start()
            finish(result_of(2, chunk), chunk)
        else:
            ready(0, chunk)
            moves[0].start()
            ready(1, chunk)
            moves[1].start()

    def back(index, chunk):
        if index == 0:
            arrived(2, chunk)
            add_in(0, in_a, chunk)
        elif index == 1:
            arrived(2, chunk)
            add_in(0, in_a, chunk)
            sends(chunk)[1][2].start()
            arrived(3, chunk)
            add_in(1, in_b, chunk)
        elif index == 3:
            arrived(2, chunk)
        if index != 2:
            finish(result_of(index, chunk), chunk)

    barrier = pltpu.get_barrier_semaphore()

    def greet(device):
        pl.semaphore_signal(barrier, inc=1, device_id={"energy": device}, device_id_type=MESH)

    greet(partner)

    @pl.when(line > 0)
    def _():
        greet(place - 2)

    @pl.when(line < 3)
    def _():
        greet(place + 2)

    inner = (line > 0) & (line < 3)

    @pl.when(inner)
    def _():
        pl.semaphore_wait(barrier, 3)

    @pl.when(jnp.logical_not(inner))
    def _():
        pl.semaphore_wait(barrier, 2)

    def start_one(chunk, carry):
        issue(chunk)
        return carry

    lax.fori_loop(0, min(WINDOW, chunks), start_one, 0)

    def role(index):
        lag = LAG + 2 if index == 0 else LAG

        def step(turn, carry):
            @pl.when(turn + WINDOW < chunks)
            def _():
                issue(turn + WINDOW)

            @pl.when(turn < chunks)
            def _():
                forward(index, turn)

            if index != 2:

                @pl.when(turn >= lag)
                def _():
                    back(index, turn - lag)

            return carry

        lax.fori_loop(0, chunks + (0 if index == 2 else lag), step, 0)

        def settle(chunk, carry):
            for which in (0, 1):
                side_copy(which, chunk).wait_send()
            for move in sends(chunk)[index]:
                move.wait_send()
            result = result_of(index, chunk)
            result_own(result, chunk).wait()
            result_copy(result, chunk).wait()
            return carry

        lax.fori_loop(0, chunks, settle, 0)

    for index in range(4):

        @pl.when(line == index)
        def _(index=index):
            role(index)


def correlate_on_line(lesser_full, greater_full):
    share, segments, _, size, width = lesser_full.shape
    chunks = segments * (size // 2) // ROWS
    block = 2 * share
    energies = share * lax.axis_size("energy")
    buffer = pltpu.VMEM((chunks, block, 2, ROWS, width), jnp.float32)
    dma = pltpu.SemaphoreType.DMA
    elements = segments * size * width
    return pl.pallas_call(
        functools.partial(exchange_kernel, 1.0 / math.sqrt(energies)),
        out_shape=jax.ShapeDtypeStruct(lesser_full.shape, jnp.float32),
        in_specs=[pl.BlockSpec(memory_space=pl.ANY)] * 2,
        out_specs=pl.BlockSpec(memory_space=pl.ANY),
        scratch_shapes=[buffer] * 6
        + [pltpu.VMEM((chunks, 4, block, 2, ROWS, width), jnp.float32)]
        + [dma((2, chunks))] * 3
        + [dma((4, chunks))] * 2
        + [dma((chunks,))] * 3,
        compiler_params=pltpu.CompilerParams(
            collective_id=0, has_side_effects=True, vmem_limit_bytes=56 * 1024 * 1024
        ),
        cost_estimate=pl.CostEstimate(
            flops=elements * 400 * 8, bytes_accessed=elements * share * 24, transcendentals=0
        ),
    )(lesser_full, greater_full)


def correlate_rows(lesser_rows, greater_rows):
    energies = lesser_rows.shape[0]
    l_re, l_im = lesser_rows[:, :, 0], lesser_rows[:, :, 1]
    g_re, g_im = greater_rows[:, :, 0], greater_rows[:, :, 1]
    scale = 1.0 / math.sqrt(energies)

    def one(shift, result):
        held = (jnp.arange(energies) + shift < energies)[:, None, None, None]
        s_re = jnp.where(held, jnp.roll(l_re, -shift, axis=0), 0.0)
        s_im = jnp.where(held, jnp.roll(l_im, -shift, axis=0), 0.0)
        real_part = jnp.sum(s_re * g_re + s_im * g_im, axis=0)
        imag_part = jnp.sum(s_im * g_re - s_re * g_im, axis=0)
        row = jnp.stack([real_part, imag_part], axis=1) * scale
        return lax.dynamic_update_index_in_dim(result, row, shift, 0)

    return lax.fori_loop(0, energies, one, jnp.zeros_like(lesser_rows))


def correlate_all(lesser_full, greater_full):
    rows = [
        lax.all_to_all(array, "energy", split_axis=3, concat_axis=0, tiled=True)
        for array in (lesser_full, greater_full)
    ]
    return lax.all_to_all(
        correlate_rows(*rows), "energy", split_axis=0, concat_axis=3, tiled=True
    )


def on_device(lesser, greater, coupling_low, coupling_up):
    transfer = chain(coupling_low, coupling_up)
    lesser_full = lesser + transfer
    greater_full = jnp.stack(
        [greater[:, :, 0] + transfer[:, :, 0], greater[:, :, 1] - transfer[:, :, 1]], axis=2
    )
    if lax.axis_size("energy") == 8:
        polarization = correlate_on_line(lesser_full, greater_full)
    else:
        polarization = correlate_all(lesser_full, greater_full)
    return (polarization, lesser_full)


def solution(mesh):
    spec = P("energy", "seg", None, None, None)
    return jax.shard_map(
        on_device,
        mesh=mesh,
        in_specs=(spec, spec, spec, spec),
        out_specs=(spec, spec),
        check_vma=False,
    )
```

time: 548 us -> 314 us (0.57)
  the two profiles are of different devices: /device:TPU:2 before, /device:TPU:0 now
where the time goes in v1:
time: 314 us
  Pallas kernels  216 us (69%)
  matrix products  32.4 us (10%)
  waiting for transfers between devices  20.7 us (7%)
  other arithmetic  16.1 us (5%)
  starting transfers between devices  14.5 us (5%)
  local copies, waits for them, and re-layouts  13.8 us (4%)
    pallas_call x1, Pallas kernels, correlate_on_line(): pl.pallas_call(functools.partial(exchange_kernel, 1.0 / math.sqrt(energie...  216 us
    dot_general x32, matrix products, multiply(): jnp.einsum('...ij,...jk->...ik', one_part, two_part, precision=lax.Precis...  32.4 us
    ppermute x1, waiting for transfers between devices, chain(): to_outer = lax.ppermute(pair[:half], 'seg', [(1, 3), (2, 0)])  14.3 us
    ppermute x2, starting transfers between devices, swap_pairs(): return lax.ppermute(part, 'seg', [(0, 1), (1, 0), (2, 3), (3, 2)])  11.6 us
    unnamed x29, local copies, waits for them, and re-layouts  9.37 us
    ppermute x2, waiting for transfers between devices, swap_pairs(): return lax.ppermute(part, 'seg', [(0, 1), (1, 0), (2, 3), (3, 2)])  6.41 us
  transfers between devices with their start and end apart: 4, of which 3 were waited for; matrix products, arithmetic and copies ran while one was open for 0% of the time, Pallas kernels for 0%

profile of v1, /device:TPU:0, one launch (start us, length us, event | category | flops | bytes accessed | tf_op | source)
XLA Modules:
  0.0 314.0 jit_solution(4984575592149416539)
XLA Ops:
  0.7 4.4 %fusion.52 = (f32[4,1,2,256,256]{4,3,2,1,0:T(8,128)S(1)}, f32[4,1,2,256,256]{4,3,2,1,0:T(8,128)S(1)}, f32[4,1,2,256,256]{4,3,2,1,0:T(8,128)S(1)}, f32[4,1,2,256,256]{4,3,2,1,0:T(8,128)S(1)}) fusion(f32[4,2,2,256,256]{4,3,2,1,0:T(8,128)} %param.6, f32[4,2,2,256,256]{4,3,2,1,0:T(8,128)} %param.7), kind=kLoop, calls=%fused_computation.110 | loop fusion | bytes 16777216 | tf_op jit(solution)/shard_map/slice | solution.py:45
  5.1 1.0 fusion.8
  6.1 2.1 fusion.30
  8.2 1.6 fusion.31
  9.9 1.7 fusion.28
  11.6 1.7 fusion.29
  13.2 3.3 %fusion.19 = f32[4,1,256,256]{3,2,0,1:T(8,128)} fusion(f32[4,256,256]{2,1,0:T(8,128)} %fusion.30, f32[4,2,256,256]{3,2,0,1:T(8,128)} %copy-done.7, f32[4,2,256,256]{3,2,0,1:T(8,128)S(1)} %get-tuple-element.19), kind=kOutput, calls=%fused_computation.56 | convolution fusion | flops 402915328 | bytes 4194304 | tf_op jit(solution)/shard_map/...ij,...jk->...ik/dot_general | solution.py:20
  16.6 1.7 fusion.20
  18.2 0.9 copy-done.6
  19.2 1.7 fusion.21
  20.9 1.7 fusion.22
  22.6 2.7 fusion.9
  25.8 3.8 %collective-permute-done = f32[4,2,256,256]{3,2,0,1:T(8,128)S(1)} collective-permute-done((f32[4,2,256,256]{3,2,0,1:T(8,128)S(1)}, f32[4,2,256,256]{3,2,0,1:T(8,128)S(1)}, u32[]{:S(2)}, u32[]{:S(2)}) %collective-permute-start) | collective-permute-done | bytes 2097184 | tf_op jit(solution)/shard_map/ppermute | solution.py:32
  30.2 0.7 fusion.33
  30.9 0.7 fusion.17
  31.7 0.7 fusion.18
  32.4 1.5 pad_maximum_fusion.6
  33.8 1.3 collective-permute-start.1
  35.1 1.6 collective-permute-start.2
  36.7 14.3 %collective-permute-done.1 = f32[2,2,256,256]{3,2,0,1:T(8,128)} collective-permute-done((f32[2,2,256,256]{3,2,0,1:T(8,128)}, f32[2,2,256,256]{3,2,0,1:T(8,128)}, u32[]{:S(2)}, u32[]{:S(2)}) %collective-permute-start.1) | collective-permute-done | bytes 1048608 | tf_op jit(solution)/shard_map/ppermute | solution.py:52
  51.0 2.4 broadcast_select_fusion.2
  53.4 11.1 %collective-permute-start.3 = (f32[2,2,256,256]{3,2,0,1:T(8,128)}, f32[2,2,256,256]{3,2,0,1:T(8,128)}, u32[]{:S(2)}, u32[]{:S(2)}) collective-permute-start(f32[2,2,256,256]{3,2,0,1:T(8,128)} %broadcast_select_fusion.2), channel_id=1, source_target_pairs={{0,1},{1,0},{2,3},{3,2},{4,5},{5,4},{6,7},{7,6},{8,9},{9,8},{10,11... | collective-permute-start | bytes 3145736 | tf_op jit(solution)/shard_map/ppermute | solution.py:32
  64.5 2.6 collective-permute-done.3
  67.1 1.7 broadcast_select_fusion
  69.5 0.7 fusion.39
  70.2 0.7 fusion.15
  71.0 0.7 fusion.16
  72.3 1.0 copy-done.2
  73.3 0.7 fusion.34
  74.0 0.7 fusion.35
  74.7 0.7 convolution_add_fusion.1
  75.4 0.7 fusion.40
  76.1 0.7 fusion.41
  78.2 0.7 convolution_subtract_fusion.1
  78.9 0.7 fusion.11
  79.6 0.7 fusion.12
  80.3 0.7 convolution_subtract_fusion.3
  81.0 0.7 fusion.42
  82.4 0.9 fusion.43
  83.3 0.7 fusion.13
  84.0 0.7 fusion.14
  85.0 2.0 copy-done.9
  87.0 2.8 fusion.lesser
  89.8 0.8 copy-done.10
  90.6 0.7 fusion.2
  91.3 2.4 pad_maximum_fusion.1.greater
  93.8 215.6 %shard_map.59 = f32[4,2,2,256,256]{4,3,2,1,0:T(8,128)} custom-call(f32[4,2,2,256,256]{4,3,2,1,0:T(8,128)} %fusion.lesser, f32[4,2,2,256,256]{4,3,2,1,0:T(8,128)} %pad_maximum_fusion.1.greater), custom_call_target="tpu_custom_call" | custom-call | flops 419430400 | bytes 12582912 | tf_op jit(solution)/shard_map/pallas_call | solution.py:396
  309.4 4.6 %copy.27 = f32[4,2,2,256,256]{4,3,2,1,0:T(8,128)} copy(f32[4,2,2,256,256]{4,3,2,1,0:T(8,128)} %shard_map.59) | data formatting | bytes 8388608
  (36 shorter events, 4.9 us)
Async XLA Ops:
  6.1 3.8 %copy-start.7 = (f32[4,2,256,256]{3,2,0,1:T(8,128)}, f32[4,2,256,256]{3,2,0,1:T(8,128)S(1)}, u32[]{:S(2)}) copy-start(f32[4,2,256,256]{3,2,0,1:T(8,128)S(1)} %get-tuple-element.18) | copy-start | bytes 6291460
  6.1 5.5 %copy-start = (f32[4,2,256,256]{3,2,0,1:T(8,128)}, f32[4,2,256,256]{3,2,0,1:T(8,128)S(1)}, u32[]{:S(2)}) copy-start(f32[4,2,256,256]{3,2,0,1:T(8,128)S(1)} %get-tuple-element.17) | copy-start | bytes 6291460
  6.1 5.5 %copy-start.5 = (f32[4,2,256,256]{3,2,0,1:T(8,128)}, f32[4,2,256,256]{3,2,0,1:T(8,128)S(1)}, u32[]{:S(2)}) copy-start(f32[4,2,256,256]{3,2,0,1:T(8,128)S(1)} %get-tuple-element.16) | copy-start | bytes 6291460
  13.2 3.3 %copy-start.8 = (f32[4,2,256,256]{3,2,0,1:T(8,128)S(1)}, f32[4,2,256,256]{3,2,0,1:T(8,128)}, u32[]{:S(2)}) copy-start(f32[4,2,256,256]{3,2,0,1:T(8,128)} %copy-done.7) | copy-start | bytes 6291460
  13.2 3.3 %copy-start.12 = (f32[4,256,256]{2,1,0:T(8,128)S(1)}, f32[4,256,256]{2,1,0:T(8,128)}, u32[]{:S(2)}) copy-start(f32[4,256,256]{2,1,0:T(8,128)} %fusion.31) | copy-start | bytes 3145732
  13.2 5.0 %copy-start.13 = (f32[4,256,256]{2,1,0:T(8,128)S(1)}, f32[4,256,256]{2,1,0:T(8,128)}, u32[]{:S(2)}) copy-start(f32[4,256,256]{2,1,0:T(8,128)} %fusion.28) | copy-start | bytes 3145732
  16.6 1.7 copy-start.1
  16.6 2.6 copy-start.6
  19.2 1.7 copy-start.11
  25.3 4.3 %collective-permute-start = (f32[4,2,256,256]{3,2,0,1:T(8,128)S(1)}, f32[4,2,256,256]{3,2,0,1:T(8,128)S(1)}, u32[]{:S(2)}, u32[]{:S(2)}) collective-permute-start(f32[4,2,256,256]{3,2,0,1:T(8,128)S(1)} %get-tuple-element.7), channel_id=1, source_target_pairs={{0,1},{1,0},{2,3},{3,2},{4,5},{5,4},{6,7},{7,6},{8,9},{9,8},{10,11... | collective-permute-start | bytes 6291464 | tf_op jit(solution)/shard_map/ppermute | solution.py:32
  29.6 2.1 copy-start.3
  33.8 17.2 %collective-permute-start.1 = (f32[2,2,256,256]{3,2,0,1:T(8,128)}, f32[2,2,256,256]{3,2,0,1:T(8,128)}, u32[]{:S(2)}, u32[]{:S(2)}) collective-permute-start(f32[2,2,256,256]{3,2,0,1:T(8,128)} %get-tuple-element.15), channel_id=1, source_target_pairs={{1,3},{2,0},{5,7},{6,4},{9,11},{10,8},{13,15},{14,12},{17,19},{18,... | collective-permute-start | bytes 3145736 | tf_op jit(solution)/shard_map/ppermute | solution.py:52
  35.1 15.9 %collective-permute-start.2 = (f32[2,2,256,256]{3,2,0,1:T(8,128)}, f32[2,2,256,256]{3,2,0,1:T(8,128)}, u32[]{:S(2)}, u32[]{:S(2)}) collective-permute-start(f32[2,2,256,256]{3,2,0,1:T(8,128)} %get-tuple-element.14), channel_id=1, source_target_pairs={{1,2},{2,1},{5,6},{6,5},{9,10},{10,9},{13,14},{14,13},{17,18},{18,... | collective-permute-start | bytes 3145736 | tf_op jit(solution)/shard_map/ppermute | solution.py:53
  53.4 13.7 %collective-permute-start.3 = (f32[2,2,256,256]{3,2,0,1:T(8,128)}, f32[2,2,256,256]{3,2,0,1:T(8,128)}, u32[]{:S(2)}, u32[]{:S(2)}) collective-permute-start(f32[2,2,256,256]{3,2,0,1:T(8,128)} %broadcast_select_fusion.2), channel_id=1, source_target_pairs={{0,1},{1,0},{2,3},{3,2},{4,5},{5,4},{6,7},{7,6},{8,9},{9,8},{10,11... | collective-permute-start | bytes 3145736 | tf_op jit(solution)/shard_map/ppermute | solution.py:32
  64.5 4.4 %copy-start.4 = (f32[4,2,256,256]{3,2,0,1:T(8,128)S(1)}, f32[4,2,256,256]{3,2,0,1:T(8,128)}, u32[]{:S(2)}) copy-start(f32[4,2,256,256]{3,2,0,1:T(8,128)} %copy-done.3) | copy-start | bytes 6291460
  71.7 1.6 copy-start.2
  84.8 2.2 copy-start.9
  87.0 3.6 %copy-start.10 = (f32[4,2,2,256,256]{4,3,2,1,0:T(8,128)S(1)}, f32[4,2,2,256,256]{4,3,2,1,0:T(8,128)}, u32[]{:S(2)}) copy-start(f32[4,2,2,256,256]{4,3,2,1,0:T(8,128)} %param.5) | copy-start | bytes 12582916

commit v2 on v1

--- a/solution.py
+++ b/solution.py
@@ -14,56 +14,191 @@
 WINDOW = 3
 
 
-def complex_product(former, latter):
-
-    def multiply(one_part, two_part):
-        return jnp.einsum("...ij,...jk->...ik", one_part, two_part, precision=lax.Precision.HIGH)
-
-    real_part = multiply(former[..., 0, :, :], latter[..., 0, :, :]) - multiply(
-        former[..., 1, :, :], latter[..., 1, :, :]
+LOW, UP, LOW_TOTAL, UP_TOTAL, PAIR, IDENTITY, NEAR, FAR, BOTH, LEFT_ONE, RIGHT_ONE, FIRST, SECOND = (
+    0, 2, 4, 5, 6, 7, 8, 9, 10, 11, 12, 13, 14,
+)
+SLOTS = 15
+
+
+def halves(value):
+    high = value.astype(jnp.bfloat16)
+    return high, (value - high.astype(jnp.float32)).astype(jnp.bfloat16)
+
+
+def off_identity_product(held, target, former, latter, energy):
+    f_re, f_im = held[former, energy, 0], held[former, energy, 1]
+    l_re, l_im = held[latter, energy, 0], held[latter, energy, 1]
+    size = f_re.shape[0]
+    f_high, f_low = halves(jnp.concatenate([f_re, f_im], axis=1))
+    l_high, l_low = halves(
+        jnp.concatenate(
+            [jnp.concatenate([l_re, l_im], axis=1), jnp.concatenate([-l_im, l_re], axis=1)], axis=0
+        )
     )
-    imag_part = multiply(former[..., 0, :, :], latter[..., 1, :, :]) + multiply(
-        former[..., 1, :, :], latter[..., 0, :, :]
-    )
-    return jnp.stack([real_part, imag_part], axis=-3)
-
-
-def swap_pairs(part):
-    return lax.ppermute(part, "seg", [(0, 1), (1, 0), (2, 3), (3, 2)])
+
+    def multiply(one, two):
+        return jnp.dot(one, two, preferred_element_type=jnp.float32)
+
+    both = multiply(f_high, l_high) + (multiply(f_high, l_low) + multiply(f_low, l_high))
+    held[target, energy, 0] = f_re + l_re + both[:, :size]
+    held[target, energy, 1] = f_im + l_im + both[:, size:]
+
+
+def chain_kernel(
+    coupling_low, coupling_up, out, held, in_sem, out_sem, near_send, near_recv, far_send, far_recv, relay_send
+):
+    energies = out.shape[0]
+    place = lax.axis_index("seg")
+    odd = place % 2
+    neighbour = place + 1 - 2 * odd
+    across = (place + 2) % 4
+    outer = (place == 0) | (place == 3)
+
+    def load(which, segment, energy):
+        source = (coupling_low, coupling_up)[which]
+        return pltpu.make_async_copy(
+            source.at[energy, segment],
+            held.at[2 * which + segment, energy],
+            in_sem.at[2 * which + segment, energy],
+        )
+
+    def store(segment, energy):
+        return pltpu.make_async_copy(
+            held.at[FIRST + segment, energy], out.at[energy, segment], out_sem.at[segment, energy]
+        )
+
+    def remote(source, target, send, recv, device):
+        return pltpu.make_async_remote_copy(
+            src_ref=source,
+            dst_ref=target,
+            send_sem=send,
+            recv_sem=recv,
+            device_id={"seg": device},
+            device_id_type=MESH,
+        )
+
+    def near(energy):
+        return remote(
+            held.at[LOW_TOTAL + odd, energy],
+            held.at[NEAR, energy],
+            near_send.at[energy],
+            near_recv.at[energy],
+            neighbour,
+        )
+
+    def far(energy):
+        return remote(
+            held.at[PAIR, energy], held.at[FAR, energy], far_send.at[energy], far_recv.at[energy], across
+        )
+
+    def relay(energy):
+        return remote(
+            held.at[FAR, energy], held.at[FAR, energy], relay_send.at[energy], far_recv.at[energy], neighbour
+        )
+
+    multiply = functools.partial(off_identity_product, held)
+
+    def each(body, count=energies):
+        def one(energy, carry):
+            body(energy)
+            return carry
+
+        lax.fori_loop(0, count, one, 0)
+
+    def load_one(energy):
+        for which in (0, 1):
+            for segment in (0, 1):
+                load(which, segment, energy).start()
+
+    each(load_one)
+    barrier = pltpu.get_barrier_semaphore()
+    for device in (neighbour, across):
+        pl.semaphore_signal(barrier, inc=1, device_id={"seg": device}, device_id_type=MESH)
+    held[IDENTITY] = jnp.zeros(held.shape[1:], jnp.float32)
+    pl.semaphore_wait(barrier, 2)
+
+    def totals(turn):
+        @pl.when(turn < energies)
+        def _():
+            for which in (0, 1):
+                for segment in (0, 1):
+                    load(which, segment, turn).wait()
+
+            multiply(LOW_TOTAL, LOW + 1, LOW, turn)
+            multiply(UP_TOTAL, UP, UP + 1, turn)
+            near(turn).start()
+
+        @pl.when(turn >= 1)
+        def _():
+            energy = turn - 1
+            near(energy).wait_recv()
+            multiply(PAIR, UP_TOTAL - odd, NEAR, energy)
+
+            @pl.when(jnp.logical_not(outer))
+            def _():
+                far(energy).start()
+
+    each(totals, energies + 1)
+
+    def finish(energy):
+        far(energy).wait_recv()
+
+        @pl.when(outer)
+        def _():
+            relay(energy).start()
+            multiply(BOTH, NEAR, FAR, energy)
+
+        left, right = IDENTITY + place, BOTH - place
+        multiply(LEFT_ONE, LOW, left, energy)
+        multiply(RIGHT_ONE, UP + 1, right, energy)
+        multiply(FIRST, left, RIGHT_ONE, energy)
+        store(0, energy).start()
+        multiply(SECOND, LEFT_ONE, right, energy)
+        store(1, energy).start()
+
+    each(finish)
+
+    def settle(energy):
+        near(energy).wait_send()
+
+        @pl.when(outer)
+        def _():
+            relay(energy).wait_send()
+
+        @pl.when(jnp.logical_not(outer))
+        def _():
+            far(energy).wait_send()
+
+        for segment in (0, 1):
+            store(segment, energy).wait()
+
+    each(settle)
 
 
 def chain(coupling_low, coupling_up):
-    place = lax.axis_index("seg")
-    even = place % 2 == 0
-    outer = (place == 0) | (place == 3)
-    energies = coupling_low.shape[0]
-    block_size = coupling_low.shape[-1]
-    eye_block = jnp.eye(block_size, dtype=jnp.float32)
-    identity = jnp.broadcast_to(
-        jnp.stack([eye_block, jnp.zeros_like(eye_block)]), (energies, 2, block_size, block_size)
-    )
-    low = [coupling_low[:, s] + identity for s in range(2)]
-    up = [coupling_up[:, s] + identity for s in range(2)]
-    low_total = complex_product(low[1], low[0])
-    up_total = complex_product(up[0], up[1])
-    near = swap_pairs(jnp.where(even, low_total, up_total))
-    pair = complex_product(jnp.where(even, up_total, low_total), near)
-    half = energies // 2
-    to_outer = lax.ppermute(pair[:half], "seg", [(1, 3), (2, 0)])
-    to_inner = lax.ppermute(pair[half:], "seg", [(1, 2), (2, 1)])
-    mine = jnp.where(outer, to_outer, to_inner)
-    other = swap_pairs(mine)
-    far = jnp.concatenate([jnp.where(outer, mine, other), jnp.where(outer, other, mine)], axis=0)
-    both = complex_product(near, far)
-    left = jnp.where(
-        place == 0, identity, jnp.where(place == 1, near, jnp.where(place == 2, far, both))
-    )
-    right = jnp.where(
-        place == 0, both, jnp.where(place == 1, far, jnp.where(place == 2, near, identity))
-    )
-    first = complex_product(left, complex_product(up[1], right))
-    second = complex_product(complex_product(low[0], left), right)
-    return jnp.stack([first, second], axis=1)
+    energies, segments, _, size, _ = coupling_low.shape
+    assert (lax.axis_size("seg"), segments) == (4, 2)
+    dma = pltpu.SemaphoreType.DMA
+    return pl.pallas_call(
+        chain_kernel,
+        out_shape=jax.ShapeDtypeStruct(coupling_low.shape, jnp.float32),
+        in_specs=[pl.BlockSpec(memory_space=pl.ANY)] * 2,
+        out_specs=pl.BlockSpec(memory_space=pl.ANY),
+        scratch_shapes=[
+            pltpu.VMEM((SLOTS, energies, 2, size, size), jnp.float32),
+            dma((4, energies)),
+            dma((2, energies)),
+        ]
+        + [dma((energies,))] * 5,
+        compiler_params=pltpu.CompilerParams(
+            collective_id=1, has_side_effects=True, vmem_limit_bytes=56 * 1024 * 1024
+        ),
+        cost_estimate=pl.CostEstimate(
+            flops=energies * 8 * 3 * 8 * size**3,
+            bytes_accessed=energies * segments * 24 * size**2,
+            transcendentals=0,
+        ),
+    )(coupling_low, coupling_up)
 
 
 def block_terms(lesser_ref, greater_ref, rows, columns, later):
@@ -219,21 +354,24 @@
         part[chunk, index] = part[chunk, index] + source[chunk]
 
     def sends(chunk):
+        def move(source, target, send, recv, device):
+            return lambda: along(source, target, send, recv, chunk, device)
+
         return (
-            (along(g_own.at[chunk], g_one.at[chunk], 0, 0, chunk, place + 2),),
+            (move(g_own.at[chunk], g_one.at[chunk], 0, 0, place + 2),),
             (
-                along(g_own.at[chunk], g_one.at[chunk], 0, 0, chunk, place + 2),
-                along(g_one.at[chunk], g_two.at[chunk], 1, 1, chunk, place + 2),
-                along(part.at[chunk, 0], in_a.at[chunk], 2, 2, chunk, place - 2),
+                move(g_own.at[chunk], g_one.at[chunk], 0, 0, place + 2),
+                move(g_one.at[chunk], g_two.at[chunk], 1, 1, place + 2),
+                move(part.at[chunk, 0], in_a.at[chunk], 2, 2, place - 2),
             ),
             (
-                along(part.at[chunk, 0], in_a.at[chunk], 0, 2, chunk, place - 2),
-                along(part.at[chunk, 1], in_b.at[chunk], 1, 3, chunk, place - 2),
-                along(part.at[chunk, 3], in_a.at[chunk], 2, 2, chunk, place + 2),
+                move(part.at[chunk, 0], in_a.at[chunk], 0, 2, place - 2),
+                move(part.at[chunk, 1], in_b.at[chunk], 1, 3, place - 2),
+                move(part.at[chunk, 3], in_a.at[chunk], 2, 2, place + 2),
             ),
             (
-                along(l_own.at[chunk], in_a.at[chunk], 0, 2, chunk, place - 2),
-                along(g_own.at[chunk], in_b.at[chunk], 1, 3, chunk, place - 2),
+                move(l_own.at[chunk], in_a.at[chunk], 0, 2, place - 2),
+                move(g_own.at[chunk], in_b.at[chunk], 1, 3, place - 2),
             ),
         )
 
@@ -247,14 +385,14 @@
         moves = sends(chunk)[index]
         if index == 0:
             ready(1, chunk)
-            moves[0].start()
+            moves[0]().start()
             ready(0, chunk)
             correlate(chunk, (0, [(l_here, g_here, False)]))
         elif index == 1:
             ready(1, chunk)
-            moves[0].start()
+            moves[0]().start()
             arrived(0, chunk)
-            moves[1].start()
+            moves[1]().start()
             ready(0, chunk)
             correlate(
                 chunk,
@@ -290,13 +428,13 @@
                 (3, [(l_next, two, False)]),
             )
             for move in moves:
-                move.start()
+                move().start()
             finish(result_of(2, chunk), chunk)
         else:
             ready(0, chunk)
-            moves[0].start()
+            moves[0]().start()
             ready(1, chunk)
-            moves[1].start()
+            moves[1]().start()
 
     def back(index, chunk):
         if index == 0:
@@ -305,7 +443,7 @@
         elif index == 1:
             arrived(2, chunk)
             add_in(0, in_a, chunk)
-            sends(chunk)[1][2].start()
+            sends(chunk)[1][2]().start()
             arrived(3, chunk)
             add_in(1, in_b, chunk)
         elif index == 3:
@@ -370,7 +508,7 @@
             for which in (0, 1):
                 side_copy(which, chunk).wait_send()
             for move in sends(chunk)[index]:
-                move.wait_send()
+                move().wait_send()
             result = result_of(index, chunk)
             result_own(result, chunk).wait()
             result_copy(result, chunk).wait()
@@ -441,11 +579,12 @@
 
 
 def on_device(lesser, greater, coupling_low, coupling_up):
-    transfer = chain(coupling_low, coupling_up)
+    size = lesser.shape[-1]
+    unit = jnp.eye(size, dtype=jnp.float32) * jnp.array([1.0, 0.0], jnp.float32)[:, None, None]
+    sign = jnp.array([1.0, -1.0], jnp.float32)[:, None, None]
+    transfer = chain(coupling_low, coupling_up) + unit
     lesser_full = lesser + transfer
-    greater_full = jnp.stack(
-        [greater[:, :, 0] + transfer[:, :, 0], greater[:, :, 1] - transfer[:, :, 1]], axis=2
-    )
+    greater_full = greater + sign * transfer
     if lax.axis_size("energy") == 8:
         polarization = correlate_on_line(lesser_full, greater_full)
     else:

time: 314 us -> 267 us (0.85)
  Pallas kernels: 216 us -> 252 us
  matrix products: 32.4 us -> 0 us
  waiting for transfers between devices: 20.7 us -> 0 us
  starting transfers between devices: 14.5 us -> 0 us
  local copies, waits for them, and re-layouts: 13.8 us -> 4.61 us
  other arithmetic: 16.1 us -> 9.01 us
    pallas_call x0 -> x1, Pallas kernels: none -> 35.6 us  [chain(): pl.pallas_call(chain_kernel, out_shape=jax.ShapeDtypeStruct(coupling_low....]
    dot_general x32 -> x0, matrix products: 32.4 us -> none  [multiply(): jnp.einsum('...ij,...jk->...ik', one_part, two_part, precision=lax.Precis...]
    ppermute x4 -> x0, waiting for transfers between devices: 20.7 us -> none  [the longest x1 14.3 us: chain(): to_outer = lax.ppermute(pair[:half], 'seg', [(1, 3), (2, 0)])]
    ppermute x4 -> x0, starting transfers between devices: 14.5 us -> none  [the longest x2 11.6 us: swap_pairs(): return lax.ppermute(part, 'seg', [(0, 1), (1, 0), (2, 3), (3, 2)])]
    select_n x4 -> x0, other arithmetic: 7.39 us -> none  [the longest x1 2.67 us: chain(): pair = complex_product(jnp.where(even, up_total, low_total), near)]
    unnamed x29 -> x5, local copies, waits for them, and re-layouts: 9.37 us -> 4.61 us
    slice x1 -> x0, local copies, waits for them, and re-layouts: 4.39 us -> none  [chain(): low = [coupling_low[:, s] + identity for s in range(2)]]
    another operation x5 -> x0, other arithmetic: 4.21 us -> none  [the longest x1 2.44 us: on_device(): jnp.stack([greater[:, :, 0] + transfer[:, :, 0], greater[:, :, 1] - trans...]
  transfers between devices with their start and end apart: 4 -> 0, of which waited for: 3 -> 0; matrix products, arithmetic and copies ran while one was open for 0% -> 0% of each run, Pallas kernels for 0% -> 0%
where the time goes in v2:
time: 267 us
  Pallas kernels  252 us (94%)
  other arithmetic  9.01 us (3%)
  local copies, waits for them, and re-layouts  4.61 us (2%)
    pallas_call x1, Pallas kernels, correlate_on_line(): pl.pallas_call(functools.partial(exchange_kernel, 1.0 / math.sqrt(energie...  217 us
    pallas_call x1, Pallas kernels, chain(): pl.pallas_call(chain_kernel, out_shape=jax.ShapeDtypeStruct(coupling_low....  35.6 us
    add x1, other arithmetic, on_device(): greater_full = greater + sign * transfer  8.23 us

profile of v2, /device:TPU:0, one launch (start us, length us, event | category | flops | bytes accessed | tf_op | source)
XLA Modules:
  0.0 266.8 jit_solution(4455029089907905269)
XLA Ops:
  0.7 0.8 broadcast_multiply_fusion
  1.4 0.0 copy-start
  1.4 0.0 copy-start.1
  1.4 35.6 %shard_map.77 = f32[4,2,2,256,256]{4,3,2,1,0:T(8,128)} custom-call(f32[4,2,2,256,256]{4,3,2,1,0:T(8,128)} %coupling_low.1, f32[4,2,2,256,256]{4,3,2,1,0:T(8,128)} %coupling_up.1), custom_call_target="tpu_custom_call" | custom-call | flops 12884901888 | bytes 12582912 | tf_op jit(solution)/shard_map/pallas_call | solution.py:182
  37.0 0.0 copy-done
  37.0 0.0 copy-done.1
  37.0 8.2 %multiply_add_fusion = (f32[4,2,2,256,256]{4,3,2,1,0:T(8,128)}, f32[4,2,2,256,256]{4,3,2,1,0:T(8,128)}) fusion(f32[4,2,2,256,256]{4,3,2,1,0:T(8,128)S(1)} %copy-done, f32[4,2,2,256,256]{4,3,2,1,0:T(8,128)} %shard_map.77, f32[2]{0:T(128)S(1)} %copy-done.1, f32[2,256,256]{2,1,0:T(8,128)S(1)} %broadcast_multiply_fusion, f32[4,2,2,256,256]{4,3,2,1,0:T(8,128)} %param.6), kind=kLoop, calls=%fused_computation | loop fusion | flops 4194304 | bytes 21495816 | tf_op jit(solution)/shard_map/add | solution.py:587
  45.3 216.9 %shard_map.78 = f32[4,2,2,256,256]{4,3,2,1,0:T(8,128)} custom-call(f32[4,2,2,256,256]{4,3,2,1,0:T(8,128)} %get-tuple-element.7.lesser, f32[4,2,2,256,256]{4,3,2,1,0:T(8,128)} %get-tuple-element.2.greater), custom_call_target="tpu_custom_call" | custom-call | flops 419430400 | bytes 12582912 | tf_op jit(solution)/shard_map/pallas_call | solution.py:534
  262.2 4.6 %copy.9 = f32[4,2,2,256,256]{4,3,2,1,0:T(8,128)} copy(f32[4,2,2,256,256]{4,3,2,1,0:T(8,128)} %shard_map.78) | data formatting | bytes 8388608
  (1 shorter events, 0.0 us)
Async XLA Ops:
  1.4 35.6 %copy-start = (f32[4,2,2,256,256]{4,3,2,1,0:T(8,128)S(1)}, f32[4,2,2,256,256]{4,3,2,1,0:T(8,128)}, u32[]{:S(2)}) copy-start(f32[4,2,2,256,256]{4,3,2,1,0:T(8,128)} %param.7) | copy-start | bytes 12582916
  1.4 35.6 %copy-start.1 = (f32[2]{0:T(128)S(1)}, f32[2]{0:T(128)}, u32[]{:S(2)}) copy-start(f32[2]{0:T(128)} %constant.5.clone) | copy-start | bytes 28

commit v3 on v2

--- a/solution.py
+++ b/solution.py
@@ -9,9 +9,9 @@
 from jax.sharding import PartitionSpec as P
 
 MESH = pl.DeviceIdType.MESH
-ROWS = 16
-LAG = 4
-WINDOW = 3
+ROWS = 8
+LAG = 6
+WINDOW = 4
 
 
 LOW, UP, LOW_TOTAL, UP_TOTAL, PAIR, IDENTITY, NEAR, FAR, BOTH, LEFT_ONE, RIGHT_ONE, FIRST, SECOND = (
@@ -45,14 +45,32 @@
 
 
 def chain_kernel(
-    coupling_low, coupling_up, out, held, in_sem, out_sem, near_send, near_recv, far_send, far_recv, relay_send
+    coupling_low,
+    coupling_up,
+    lesser,
+    greater,
+    lesser_full,
+    greater_full,
+    held,
+    full,
+    in_sem,
+    add_sem,
+    out_sem,
+    near_send,
+    near_recv,
+    far_send,
+    far_recv,
+    relay_send,
 ):
-    energies = out.shape[0]
+    energies, _, _, size, _ = lesser.shape
     place = lax.axis_index("seg")
     odd = place % 2
     neighbour = place + 1 - 2 * odd
     across = (place + 2) % 4
     outer = (place == 0) | (place == 3)
+    upper = place // 2
+    near_side = (1 - upper) * (IDENTITY + place) + upper * (BOTH - place)
+    far_side = (1 - upper) * (BOTH - place) + upper * (IDENTITY + place)
 
     def load(which, segment, energy):
         source = (coupling_low, coupling_up)[which]
@@ -62,10 +80,34 @@
             in_sem.at[2 * which + segment, energy],
         )
 
-    def store(segment, energy):
+    def load_add(which, segment, energy):
         return pltpu.make_async_copy(
-            held.at[FIRST + segment, energy], out.at[energy, segment], out_sem.at[segment, energy]
-        )
+            (lesser, greater)[which].at[energy, segment],
+            full.at[which, segment, energy],
+            add_sem.at[2 * which + segment, energy],
+        )
+
+    def store(which, segment, energy):
+        return pltpu.make_async_copy(
+            full.at[which, segment, energy],
+            (lesser_full, greater_full)[which].at[energy, segment],
+            out_sem.at[2 * which + segment, energy],
+        )
+
+    def join(segment, energy):
+        diagonal = lax.broadcasted_iota(jnp.int32, (size, size), 0) == lax.broadcasted_iota(
+            jnp.int32, (size, size), 1
+        )
+        real_part = held[FIRST + segment, energy, 0] + jnp.where(diagonal, 1.0, 0.0)
+        imag_part = held[FIRST + segment, energy, 1]
+        for which in (0, 1):
+            load_add(which, segment, energy).wait()
+        full[0, segment, energy, 0] = full[0, segment, energy, 0] + real_part
+        full[0, segment, energy, 1] = full[0, segment, energy, 1] + imag_part
+        full[1, segment, energy, 0] = full[1, segment, energy, 0] + real_part
+        full[1, segment, energy, 1] = full[1, segment, energy, 1] - imag_part
+        for which in (0, 1):
+            store(which, segment, energy).start()
 
     def remote(source, target, send, recv, device):
         return pltpu.make_async_remote_copy(
@@ -110,7 +152,13 @@
             for segment in (0, 1):
                 load(which, segment, energy).start()
 
+    def load_add_one(energy):
+        for which in (0, 1):
+            for segment in (0, 1):
+                load_add(which, segment, energy).start()
+
     each(load_one)
+    each(load_add_one)
     barrier = pltpu.get_barrier_semaphore()
     for device in (neighbour, across):
         pl.semaphore_signal(barrier, inc=1, device_id={"seg": device}, device_id_type=MESH)
@@ -138,6 +186,8 @@
             def _():
                 far(energy).start()
 
+            multiply(LEFT_ONE + upper, LOW + 3 * upper, near_side, energy)
+
     each(totals, energies + 1)
 
     def finish(energy):
@@ -148,13 +198,11 @@
             relay(energy).start()
             multiply(BOTH, NEAR, FAR, energy)
 
-        left, right = IDENTITY + place, BOTH - place
-        multiply(LEFT_ONE, LOW, left, energy)
-        multiply(RIGHT_ONE, UP + 1, right, energy)
-        multiply(FIRST, left, RIGHT_ONE, energy)
-        store(0, energy).start()
-        multiply(SECOND, LEFT_ONE, right, energy)
-        store(1, energy).start()
+        multiply(RIGHT_ONE - upper, LOW + 3 * (1 - upper), far_side, energy)
+        multiply(FIRST, IDENTITY + place, RIGHT_ONE, energy)
+        join(0, energy)
+        multiply(SECOND, LEFT_ONE, BOTH - place, energy)
+        join(1, energy)
 
     each(finish)
 
@@ -169,36 +217,67 @@
         def _():
             far(energy).wait_send()
 
-        for segment in (0, 1):
-            store(segment, energy).wait()
+        for which in (0, 1):
+            for segment in (0, 1):
+                store(which, segment, energy).wait()
 
     each(settle)
 
 
-def chain(coupling_low, coupling_up):
+def chain(coupling_low, coupling_up, lesser, greater):
     energies, segments, _, size, _ = coupling_low.shape
     assert (lax.axis_size("seg"), segments) == (4, 2)
     dma = pltpu.SemaphoreType.DMA
     return pl.pallas_call(
         chain_kernel,
-        out_shape=jax.ShapeDtypeStruct(coupling_low.shape, jnp.float32),
-        in_specs=[pl.BlockSpec(memory_space=pl.ANY)] * 2,
-        out_specs=pl.BlockSpec(memory_space=pl.ANY),
+        out_shape=[jax.ShapeDtypeStruct(lesser.shape, jnp.float32)] * 2,
+        in_specs=[pl.BlockSpec(memory_space=pl.ANY)] * 4,
+        out_specs=[pl.BlockSpec(memory_space=pl.ANY)] * 2,
         scratch_shapes=[
             pltpu.VMEM((SLOTS, energies, 2, size, size), jnp.float32),
-            dma((4, energies)),
-            dma((2, energies)),
+            pltpu.VMEM((2, segments, energies, 2, size, size), jnp.float32),
         ]
+        + [dma((4, energies))] * 3
         + [dma((energies,))] * 5,
         compiler_params=pltpu.CompilerParams(
             collective_id=1, has_side_effects=True, vmem_limit_bytes=56 * 1024 * 1024
         ),
         cost_estimate=pl.CostEstimate(
             flops=energies * 8 * 3 * 8 * size**3,
-            bytes_accessed=energies * segments * 24 * size**2,
+            bytes_accessed=energies * segments * 48 * size**2,
             transcendentals=0,
         ),
-    )(coupling_low, coupling_up)
+    )(coupling_low, coupling_up, lesser, greater)
+
+
+def hand_on_kernel(one, two, one_out, two_out, sem):
+    copies = [
+        pltpu.make_async_copy(source.at[piece], target.at[piece], sem.at[which, piece])
+        for piece in range(one.shape[0])
+        for which, (source, target) in enumerate(((one, one_out), (two, two_out)))
+    ]
+    for copy in copies:
+        copy.start()
+    for copy in copies:
+        copy.wait()
+
+
+def hand_on(one, two):
+    shape = one.shape
+    pieces = shape[0] * shape[1]
+    flat = (pieces, *shape[2:])
+    results = pl.pallas_call(
+        hand_on_kernel,
+        out_shape=[jax.ShapeDtypeStruct(flat, jnp.float32)] * 2,
+        in_specs=[pl.BlockSpec(memory_space=pl.ANY)] * 2,
+        out_specs=[pl.BlockSpec(memory_space=pl.ANY)] * 2,
+        scratch_shapes=[pltpu.SemaphoreType.DMA((2, pieces))],
+        compiler_params=pltpu.CompilerParams(vmem_limit_bytes=16 * 1024 * 1024),
+        cost_estimate=pl.CostEstimate(
+            flops=0, bytes_accessed=16 * math.prod(shape), transcendentals=0
+        ),
+    )(one.reshape(flat), two.reshape(flat))
+    return tuple(result.reshape(shape) for result in results)
 
 
 def block_terms(lesser_ref, greater_ref, rows, columns, later):
@@ -579,17 +658,12 @@
 
 
 def on_device(lesser, greater, coupling_low, coupling_up):
-    size = lesser.shape[-1]
-    unit = jnp.eye(size, dtype=jnp.float32) * jnp.array([1.0, 0.0], jnp.float32)[:, None, None]
-    sign = jnp.array([1.0, -1.0], jnp.float32)[:, None, None]
-    transfer = chain(coupling_low, coupling_up) + unit
-    lesser_full = lesser + transfer
-    greater_full = greater + sign * transfer
+    lesser_full, greater_full = chain(coupling_low, coupling_up, lesser, greater)
     if lax.axis_size("energy") == 8:
         polarization = correlate_on_line(lesser_full, greater_full)
     else:
         polarization = correlate_all(lesser_full, greater_full)
-    return (polarization, lesser_full)
+    return hand_on(polarization, lesser_full)
 
 
 def solution(mesh):

time: 267 us -> 251 us (0.940)
  other arithmetic: 9.01 us -> 0 us
  Pallas kernels: 252 us -> 248 us
    add x1 -> x0, other arithmetic: 8.23 us -> none  [on_device(): greater_full = greater + sign * transfer]
    pallas_call x1, Pallas kernels: 217 us -> 209 us  [correlate_on_line(): pl.pallas_call(functools.partial(exchange_kernel, 1.0 / math.sqrt(energie...]
    pallas_call x1 -> x2, Pallas kernels: 35.6 us -> 39.1 us  [the longest x1 35.7 us: chain(): pl.pallas_call(chain_kernel, out_shape=[jax.ShapeDtypeStruct(lesser.shape...]
where the time goes in v3:
time: 251 us
  Pallas kernels  248 us (99%)
    pallas_call x1, Pallas kernels, correlate_on_line(): pl.pallas_call(functools.partial(exchange_kernel, 1.0 / math.sqrt(energie...  209 us
    pallas_call x1, Pallas kernels, chain(): pl.pallas_call(chain_kernel, out_shape=[jax.ShapeDtypeStruct(lesser.shape...  35.7 us

profile of v3, /device:TPU:0, one launch (start us, length us, event | category | flops | bytes accessed | tf_op | source)
XLA Modules:
  0.0 251.2 jit_solution(490142413452748392)
XLA Ops:
  0.6 35.7 %shard_map.59 = (f32[4,2,2,256,256]{4,3,2,1,0:T(8,128)}, f32[4,2,2,256,256]{4,3,2,1,0:T(8,128)}) custom-call(f32[4,2,2,256,256]{4,3,2,1,0:T(8,128)} %coupling_low.1, f32[4,2,2,256,256]{4,3,2,1,0:T(8,128)} %coupling_up.1, f32[4,2,2,256,256]{4,3,2,1,0:T(8,128)} %lesser.1, f32[4,2,2,256,256]{4,3,2,1,0:T(8,128)} %greater.1), custom_call_target="tpu_custom_call" | custom-call | flops 12884901888 | bytes 25165824 | tf_op jit(solution)/shard_map/pallas_call | solution.py:231
  36.3 0.0 copy-start
  36.3 209.2 %shard_map.60 = f32[4,2,2,256,256]{4,3,2,1,0:T(8,128)} custom-call(f32[4,2,2,256,256]{4,3,2,1,0:T(8,128)} %get-tuple-element.6.lesser, f32[4,2,2,256,256]{4,3,2,1,0:T(8,128)} %get-tuple-element.7.greater), custom_call_target="tpu_custom_call" | custom-call | flops 419430400 | bytes 12582912 | tf_op jit(solution)/shard_map/pallas_call | solution.py:613
  245.6 0.0 copy-done
  245.6 0.0 copy-start.1
  245.6 2.2 copy-done.1
  247.8 3.4 %shard_map.61 = (f32[8,2,256,256]{3,2,1,0:T(8,128)}, f32[8,2,256,256]{3,2,1,0:T(8,128)}) custom-call(f32[8,2,256,256]{3,2,1,0:T(8,128)S(1)} %bitcast.5, f32[8,2,256,256]{3,2,1,0:T(8,128)S(1)} %bitcast.4), custom_call_target="tpu_custom_call" | custom-call | bytes 16777216 | tf_op jit(solution)/shard_map/pallas_call | solution.py:269
Async XLA Ops:
  36.3 209.3 %copy-start = (f32[4,2,2,256,256]{4,3,2,1,0:T(8,128)S(1)}, f32[4,2,2,256,256]{4,3,2,1,0:T(8,128)}, u32[]{:S(2)}) copy-start(f32[4,2,2,256,256]{4,3,2,1,0:T(8,128)} %get-tuple-element.6.lesser) | copy-start | bytes 12582916
  245.6 2.2 copy-start.1

commit v4 on v3

--- a/solution.py
+++ b/solution.py
@@ -11,7 +11,9 @@
 MESH = pl.DeviceIdType.MESH
 ROWS = 8
 LAG = 6
-WINDOW = 4
+WINDOW = 2
+FLIGHT = 2
+AHEAD = (1, 2, 0, 2)
 
 
 LOW, UP, LOW_TOTAL, UP_TOTAL, PAIR, IDENTITY, NEAR, FAR, BOTH, LEFT_ONE, RIGHT_ONE, FIRST, SECOND = (
@@ -462,6 +464,12 @@
         one, two = g_one.at[chunk], g_two.at[chunk]
         l_next, g_next = in_a.at[chunk], in_b.at[chunk]
         moves = sends(chunk)[index]
+
+        @pl.when(chunk >= FLIGHT)
+        def _():
+            for move in sends(chunk - FLIGHT)[index][: AHEAD[index]]:
+                move().wait_send()
+
         if index == 0:
             ready(1, chunk)
             moves[0]().start()
@@ -483,31 +491,26 @@
             ready(0, chunk)
             for recv in (2, 3, 0, 1):
                 arrived(recv, chunk)
-            correlate(
-                chunk,
-                (
-                    0,
-                    [
-                        (l_here, g_here, False),
-                        (l_next, g_next, False),
-                        (l_here, one, True),
-                        (l_next, g_here, True),
-                    ],
-                ),
-                (
-                    1,
-                    [
-                        (l_here, one, False),
-                        (l_next, g_here, False),
-                        (l_here, two, True),
-                        (l_next, one, True),
-                    ],
-                ),
-                (2, [(l_here, two, False), (l_next, one, False), (l_next, two, True)]),
-                (3, [(l_next, two, False)]),
+            sums = (
+                [
+                    (l_here, g_here, False),
+                    (l_next, g_next, False),
+                    (l_here, one, True),
+                    (l_next, g_here, True),
+                ],
+                [
+                    (l_here, one, False),
+                    (l_next, g_here, False),
+                    (l_here, two, True),
+                    (l_next, one, True),
+                ],
+                [(l_here, two, False), (l_next, one, False), (l_next, two, True)],
+                [(l_next, two, False)],
             )
-            for move in moves:
-                move().start()
+            for target, start in ((0, moves[0]), (1, moves[1]), (3, moves[2])):
+                correlate(chunk, (target, sums[target]))
+                start().start()
+            correlate(chunk, (2, sums[2]))
             finish(result_of(2, chunk), chunk)
         else:
             ready(0, chunk)
@@ -586,8 +589,15 @@
         def settle(chunk, carry):
             for which in (0, 1):
                 side_copy(which, chunk).wait_send()
-            for move in sends(chunk)[index]:
+            moves = sends(chunk)[index]
+            for move in moves[AHEAD[index] :]:
                 move().wait_send()
+
+            @pl.when(chunk >= chunks - FLIGHT)
+            def _():
+                for move in moves[: AHEAD[index]]:
+                    move().wait_send()
+
             result = result_of(index, chunk)
             result_own(result, chunk).wait()
             result_copy(result, chunk).wait()

time: 251 us -> 251 us (level)
  no operation moved by 1% of the time
where the time goes in v4:
time: 251 us
  Pallas kernels  248 us (99%)
    pallas_call x1, Pallas kernels, correlate_on_line(): pl.pallas_call(functools.partial(exchange_kernel, 1.0 / math.sqrt(energie...  209 us
    pallas_call x1, Pallas kernels, chain(): pl.pallas_call(chain_kernel, out_shape=[jax.ShapeDtypeStruct(lesser.shape...  35.7 us

profile of v4, /device:TPU:0, one launch (start us, length us, event | category | flops | bytes accessed | tf_op | source)
XLA Modules:
  0.0 250.6 jit_solution(2331562211035270935)
XLA Ops:
  0.6 35.7 %shard_map.59 = (f32[4,2,2,256,256]{4,3,2,1,0:T(8,128)}, f32[4,2,2,256,256]{4,3,2,1,0:T(8,128)}) custom-call(f32[4,2,2,256,256]{4,3,2,1,0:T(8,128)} %coupling_low.1, f32[4,2,2,256,256]{4,3,2,1,0:T(8,128)} %coupling_up.1, f32[4,2,2,256,256]{4,3,2,1,0:T(8,128)} %lesser.1, f32[4,2,2,256,256]{4,3,2,1,0:T(8,128)} %greater.1), custom_call_target="tpu_custom_call" | custom-call | flops 12884901888 | bytes 25165824 | tf_op jit(solution)/shard_map/pallas_call | solution.py:233
  36.3 0.0 copy-start
  36.3 208.6 %shard_map.60 = f32[4,2,2,256,256]{4,3,2,1,0:T(8,128)} custom-call(f32[4,2,2,256,256]{4,3,2,1,0:T(8,128)} %get-tuple-element.6.lesser, f32[4,2,2,256,256]{4,3,2,1,0:T(8,128)} %get-tuple-element.7.greater), custom_call_target="tpu_custom_call" | custom-call | flops 419430400 | bytes 12582912 | tf_op jit(solution)/shard_map/pallas_call | solution.py:623
  245.0 0.0 copy-done
  245.0 0.0 copy-start.1
  245.0 2.2 copy-done.1
  247.2 3.4 %shard_map.61 = (f32[8,2,256,256]{3,2,1,0:T(8,128)}, f32[8,2,256,256]{3,2,1,0:T(8,128)}) custom-call(f32[8,2,256,256]{3,2,1,0:T(8,128)S(1)} %bitcast.5, f32[8,2,256,256]{3,2,1,0:T(8,128)S(1)} %bitcast.4), custom_call_target="tpu_custom_call" | custom-call | bytes 16777216 | tf_op jit(solution)/shard_map/pallas_call | solution.py:271
Async XLA Ops:
  36.3 208.7 %copy-start = (f32[4,2,2,256,256]{4,3,2,1,0:T(8,128)S(1)}, f32[4,2,2,256,256]{4,3,2,1,0:T(8,128)}, u32[]{:S(2)}) copy-start(f32[4,2,2,256,256]{4,3,2,1,0:T(8,128)} %get-tuple-element.6.lesser) | copy-start | bytes 12582916
  245.0 2.2 copy-start.1

commit v5 on v4

--- a/solution.py
+++ b/solution.py
@@ -10,9 +10,10 @@
 
 MESH = pl.DeviceIdType.MESH
 ROWS = 8
-LAG = 6
-WINDOW = 2
-FLIGHT = 2
+COLUMNS = 128
+LAG = 10
+WINDOW = 4
+FLIGHT = 4
 AHEAD = (1, 2, 0, 2)
 
 
@@ -342,14 +343,17 @@
     share = block // 2
     per_segment = chunks // lesser.shape[1]
     half_rows = lesser.shape[3] // 2
+    across = lesser.shape[4] // width
     place = lax.axis_index("energy")
     line = place // 2
     side = place % 2
     partner = place + 1 - 2 * side
 
     def region(ref, chunk, half):
-        start = pl.multiple_of(half * half_rows + (chunk % per_segment) * rows, rows)
-        return ref.at[:, chunk // per_segment, :, pl.ds(start, rows), :]
+        within = chunk % per_segment
+        row = pl.multiple_of(half * half_rows + (within // across) * rows, rows)
+        column = pl.multiple_of((within % across) * width, width)
+        return ref.at[:, chunk // per_segment, :, pl.ds(row, rows), pl.ds(column, width)]
 
     def remote(source, target, send, recv, device):
         return pltpu.make_async_remote_copy(
@@ -614,10 +618,10 @@
 
 def correlate_on_line(lesser_full, greater_full):
     share, segments, _, size, width = lesser_full.shape
-    chunks = segments * (size // 2) // ROWS
+    chunks = segments * (size // 2 // ROWS) * (width // COLUMNS)
     block = 2 * share
     energies = share * lax.axis_size("energy")
-    buffer = pltpu.VMEM((chunks, block, 2, ROWS, width), jnp.float32)
+    buffer = pltpu.VMEM((chunks, block, 2, ROWS, COLUMNS), jnp.float32)
     dma = pltpu.SemaphoreType.DMA
     elements = segments * size * width
     return pl.pallas_call(
@@ -626,7 +630,7 @@
         in_specs=[pl.BlockSpec(memory_space=pl.ANY)] * 2,
         out_specs=pl.BlockSpec(memory_space=pl.ANY),
         scratch_shapes=[buffer] * 6
-        + [pltpu.VMEM((chunks, 4, block, 2, ROWS, width), jnp.float32)]
+        + [pltpu.VMEM((chunks, 4, block, 2, ROWS, COLUMNS), jnp.float32)]
         + [dma((2, chunks))] * 3
         + [dma((4, chunks))] * 2
         + [dma((chunks,))] * 3,

time: 251 us -> 252 us (level)
  no operation moved by 1% of the time
where the time goes in v5:
time: 252 us; the launch traced here: 251 us
  Pallas kernels  249 us (99%)
    pallas_call x1, Pallas kernels, correlate_on_line(): pl.pallas_call(functools.partial(exchange_kernel, 1.0 / math.sqrt(energie...  209 us
    pallas_call x1, Pallas kernels, chain(): pl.pallas_call(chain_kernel, out_shape=[jax.ShapeDtypeStruct(lesser.shape...  35.7 us

profile of v5, /device:TPU:0, one launch (start us, length us, event | category | flops | bytes accessed | tf_op | source)
XLA Modules:
  0.0 251.4 jit_solution(9586657051436007513)
XLA Ops:
  0.6 35.7 %shard_map.59 = (f32[4,2,2,256,256]{4,3,2,1,0:T(8,128)}, f32[4,2,2,256,256]{4,3,2,1,0:T(8,128)}) custom-call(f32[4,2,2,256,256]{4,3,2,1,0:T(8,128)} %coupling_low.1, f32[4,2,2,256,256]{4,3,2,1,0:T(8,128)} %coupling_up.1, f32[4,2,2,256,256]{4,3,2,1,0:T(8,128)} %lesser.1, f32[4,2,2,256,256]{4,3,2,1,0:T(8,128)} %greater.1), custom_call_target="tpu_custom_call" | custom-call | flops 12884901888 | bytes 25165824 | tf_op jit(solution)/shard_map/pallas_call | solution.py:234
  36.3 0.0 copy-start
  36.3 209.5 %shard_map.60 = f32[4,2,2,256,256]{4,3,2,1,0:T(8,128)} custom-call(f32[4,2,2,256,256]{4,3,2,1,0:T(8,128)} %get-tuple-element.6.lesser, f32[4,2,2,256,256]{4,3,2,1,0:T(8,128)} %get-tuple-element.7.greater), custom_call_target="tpu_custom_call" | custom-call | flops 419430400 | bytes 12582912 | tf_op jit(solution)/shard_map/pallas_call | solution.py:627
  245.8 0.0 copy-done
  245.8 0.0 copy-start.1
  245.8 2.2 copy-done.1
  248.0 3.4 %shard_map.61 = (f32[8,2,256,256]{3,2,1,0:T(8,128)}, f32[8,2,256,256]{3,2,1,0:T(8,128)}) custom-call(f32[8,2,256,256]{3,2,1,0:T(8,128)S(1)} %bitcast.5, f32[8,2,256,256]{3,2,1,0:T(8,128)S(1)} %bitcast.4), custom_call_target="tpu_custom_call" | custom-call | bytes 16777216 | tf_op jit(solution)/shard_map/pallas_call | solution.py:272
Async XLA Ops:
  36.3 209.5 %copy-start = (f32[4,2,2,256,256]{4,3,2,1,0:T(8,128)S(1)}, f32[4,2,2,256,256]{4,3,2,1,0:T(8,128)}, u32[]{:S(2)}) copy-start(f32[4,2,2,256,256]{4,3,2,1,0:T(8,128)} %get-tuple-element.6.lesser) | copy-start | bytes 12582916
  245.8 2.2 copy-start.1
